TPU v7x, 32 devices: a whole 2x2x4 slice. The times are simulated.
32 devices in a mesh: hi: 4 (over y, core), lo: 8 (over z, x).
Axes of the slice: x: 2, y: 2, z: 4, core: 2. Of those that a mesh axis runs over, the one named last changes fastest.
Arguments:
- panel: float32 [262144, 128], P(('hi', 'lo')), may hold values from -6 to 6
- row_signs: float32 [262144, 1], P(('hi', 'lo')), may hold values from -4 to 4
- sample_rows: int32 [1024], replicated, may hold values from 0 to 262143, as said below
Outputs:
- sketch: float32 [1024, 128], P(('hi', 'lo'))
Inputs may be any that keep to these rules, and one draw needn't show every extreme that they name: `sample_rows`: repeats may occur; they fall very unevenly on the devices that hold the rows.
All inputs are finite; a program needn't handle non-finite values.
Results may differ from a plain program's by a relative error of at most 0.000098.
Values sent between devices are 32-bit elements; how exact they have to be, the bound alone decides.
A program may use at most 64 MiB of HBM per device.

v0:
```python
import functools
import math

import jax
import jax.numpy as jnp
from jax import lax
from jax.experimental import pallas as pl
from jax.experimental.pallas import tpu as pltpu
from jax.sharding import PartitionSpec as P

MESH = pl.DeviceIdType.MESH
LOW = 256
LANES = 128
TILE = 8


def parity_sign(bits):
    shift = 16
    while shift:
        bits = bits ^ (bits >> shift)
        shift //= 2
    return (1 - 2 * (bits & 1)).astype(jnp.float32)


def kernel(hi_count, lo_count, panel_hbm, signs_hbm, rows_hbm, picks_hbm, out_ref,
           panel, signs_ref, rows_ref, picks_ref, field, had, sgn, terms, mine, got_a, got_b, got_c, last,
           load_sem, small_sem, send_a, recv_a, send_b, recv_b, send_c, recv_c):
    count = panel.shape[0]
    blocks = count // LOW
    share = out_ref.shape[0]
    total = count * hi_count * lo_count
    side = 2 ** ((lo_count.bit_length() - 1) // 2)
    depth = lo_count // side
    plane = (hi_count // 2) * side
    hi, lo = lax.axis_index("hi"), lax.axis_index("lo")
    me = hi * lo_count + lo
    core = hi % 2
    spot = (hi // 2) * side + lo % side
    level = lo // side

    def place(core_to, level_to, spot_to):
        return ((spot_to // side) * 2 + core_to, level_to * side + spot_to % side)

    partner = place(1 - core, level, spot)
    peers_plane = [place(core, level, spot ^ j) for j in range(plane)]
    peers_depth = [place(core, level ^ r, spot) for r in range(depth)]

    loads = load_sem.shape[0]
    rows_load = count // loads
    small = [pltpu.make_async_copy(signs_hbm, signs_ref, small_sem.at[0]),
             pltpu.make_async_copy(picks_hbm, picks_ref, small_sem.at[1]),
             pltpu.make_async_copy(rows_hbm, rows_ref, small_sem.at[2])]
    for copy in small:
        copy.start()

    def load(i):
        part = pl.ds(i * rows_load, rows_load)
        return pltpu.make_async_copy(panel_hbm.at[part], panel.at[part], load_sem.at[i])

    for i in range(loads):
        load(i).start()

    barrier = pltpu.get_barrier_semaphore()
    greet = [partner] + peers_plane[1:] + peers_depth[1:]
    for device in greet:
        pl.semaphore_signal(barrier, inc=1, device_id=device, device_id_type=MESH)

    left = lax.broadcasted_iota(jnp.int32, (LOW, LOW), 0)
    right = lax.broadcasted_iota(jnp.int32, (LOW, LOW), 1)
    had[...] = parity_sign(left & right).astype(jnp.bfloat16)

    for copy in small:
        copy.wait()

    weight = parity_sign((picks_ref[...] // count) & me) * (1.0 / math.sqrt(total))
    for g in range(weight.shape[0]):
        sgn[pl.ds(g * LANES, LANES), :] = jnp.broadcast_to(weight[g:g + 1, :], (LANES, LANES)).T

    @pl.loop(0, loads)
    def _(i):
        load(i).wait()
        for step in range(blocks // loads):
            a = i * (blocks // loads) + step
            parts = []
            for h in range(LOW // LANES):
                line = signs_ref[pl.ds(a * (LOW // LANES) + h, 1), :]
                wide = jnp.broadcast_to(line, (LANES, LANES)).T
                parts.append(panel[pl.ds(a * LOW + h * LANES, LANES), :] * wide)
            block = jnp.concatenate(parts, axis=0)
            big = block.astype(jnp.bfloat16)
            small = (block - big.astype(jnp.float32)).astype(jnp.bfloat16)
            both = jnp.concatenate([big, small], axis=1)
            done = jnp.dot(had[...], both, preferred_element_type=jnp.float32)
            field[pl.ds(a * LOW, LOW), :] = done[:, :LANES] + done[:, LANES:]

    @pl.loop(0, LOW // TILE)
    def _(p):
        parts = [field[pl.ds(b * LOW + p * TILE, TILE), :] for b in range(blocks)]
        half = 1
        while half < blocks:
            for b in range(blocks):
                if not b & half:
                    x, y = parts[b], parts[b + half]
                    parts[b], parts[b + half] = x + y, x - y
            half *= 2
        for b in range(blocks):
            field[pl.ds(b * LOW + p * TILE, TILE), :] = parts[b]

    pl.semaphore_wait(barrier, len(greet))

    def gather(dst, core_to, level_to):
        @pl.loop(0, plane)
        def _(j):
            hi_to, lo_to = place(core_to, level_to, spot ^ j)
            start = (hi_to * lo_count + lo_to) * share
            for s in range(share):
                row = rows_ref[start + s] & (count - 1)
                dst[pl.ds(j * share + s, 1), :] = field[pl.ds(row, 1), :]
            part = pl.ds(j * share, share)
            dst[part, :] = dst[part, :] * sgn[pl.ds(start, share), :]

    def remote(src, dst, send, recv, device):
        return pltpu.make_async_remote_copy(
            src_ref=src, dst_ref=dst, send_sem=send, recv_sem=recv,
            device_id=device, device_id_type=MESH)

    levels = range(depth)
    sent_a, sent_b = {}, {}

    def send_pair(c):
        gather(terms.at[c], 1 - core, c)
        sent_a[c] = remote(terms.at[c], got_a.at[c], send_a.at[c], recv_a.at[c], partner)
        sent_a[c].start()
        if c:
            send_plane(c - 1)
        gather(mine.at[c], core, c)

    def send_plane(c):
        sent_a[c].wait_recv()
        for j in list(range(1, plane)) + [0]:
            part = pl.ds(j * share, share)
            mine[c, part, :] = mine[c, part, :] + got_a[c, part, :]
            if j:
                sent_b[c, j] = remote(mine.at[c, part], got_b.at[c, part],
                                      send_b.at[c, j], recv_b.at[c, j], peers_plane[j])
                sent_b[c, j].start()

    def to_level(c):
        return remote(last.at[c], got_c.at[level], send_c.at[c], recv_c.at[level],
                      place(core, c, spot))

    def send_level(c):
        rows = mine[c, pl.ds(0, share), :]
        for j in range(1, plane):
            sent_b[c, j].wait_recv()
            rows = rows + got_b[c, pl.ds(j * share, share), :]
        last[c] = rows

        @pl.when(level != c)
        def _():
            to_level(c).start()

    for c in levels:
        send_pair(c)
    send_plane(depth - 1)
    for c in levels:
        send_level(c)
    result = last[level]
    for r in range(1, depth):
        other = level ^ r
        remote(last.at[other], got_c.at[other], send_c.at[other], recv_c.at[other],
               place(core, other, spot)).wait_recv()
        result = result + got_c[other]
    out_ref[...] = result
    for c in levels:
        sent_a[c].wait_send()
        for j in range(1, plane):
            sent_b[c, j].wait_send()

        @pl.when(level != c)
        def _():
            to_level(c).wait_send()


def body(panel, row_signs, sample_rows):
    count, width = panel.shape
    hi_count, lo_count = lax.axis_size("hi"), lax.axis_size("lo")
    kept = sample_rows.shape[0]
    share = kept // (hi_count * lo_count)
    side = 2 ** ((lo_count.bit_length() - 1) // 2)
    depth = lo_count // side
    plane = (hi_count // 2) * side
    loads = 2
    vmem = pl.BlockSpec(memory_space=pltpu.VMEM)
    dma = pltpu.SemaphoreType.DMA
    f32 = jnp.float32
    chunk = (depth, plane * share, width)
    return pl.pallas_call(
        functools.partial(kernel, hi_count, lo_count),
        out_shape=jax.ShapeDtypeStruct((share, width), f32),
        in_specs=[pl.BlockSpec(memory_space=pltpu.HBM)] * 4,
        out_specs=vmem,
        scratch_shapes=[
            pltpu.VMEM((count, width), f32),
            pltpu.VMEM((count // LANES, LANES), f32),
            pltpu.SMEM((kept,), jnp.int32),
            pltpu.VMEM((kept // LANES, LANES), jnp.int32),
            pltpu.VMEM((count, width), f32),
            pltpu.VMEM((LOW, LOW), jnp.bfloat16),
            pltpu.VMEM((kept, width), f32),
            pltpu.VMEM(chunk, f32),
            pltpu.VMEM(chunk, f32),
            pltpu.VMEM(chunk, f32),
            pltpu.VMEM(chunk, f32),
            pltpu.VMEM((depth, share, width), f32),
            pltpu.VMEM((depth, share, width), f32),
            dma((loads,)), dma((3,)),
            dma((depth,)), dma((depth,)),
            dma((depth, plane)), dma((depth, plane)),
            dma((depth,)), dma((depth,)),
        ],
        compiler_params=pltpu.CompilerParams(
            collective_id=0, has_side_effects=True, vmem_limit_bytes=60 * 2**20),
        cost_estimate=pl.CostEstimate(
            flops=2 * count * LOW * 2 * width, bytes_accessed=count * width * 4, transcendentals=0),
    )(panel, row_signs.reshape(count // LANES, LANES), sample_rows,
      sample_rows.reshape(kept // LANES, LANES))


def solution(mesh):
    placed = (P(("hi", "lo"), None), P(("hi", "lo"), None), P())
    return jax.shard_map(
        body, mesh=mesh, in_specs=placed, out_specs=P(("hi", "lo"), None), check_vma=False
    )
```

profile of v0, /device:TPU:0, one launch (start us, length us, event | category | flops | bytes accessed | tf_op | source)
XLA Modules:
  0.0 19.3 jit_solution(12939989003301019752)
XLA Ops:
  0.0 18.0 %shard_map.37 = f32[32,128]{1,0:T(8,128)} custom-call(f32[8192,128]{1,0:T(8,128)} %panel_hbm.1, f32[64,128]{1,0:T(8,128)} %bitcast.2, s32[1024]{0:T(1024)} %rows_hbm.1, s32[8,128]{1,0:T(8,128)} %bitcast.3), custom_call_target="tpu_custom_call" | custom-call | flops 1073741824 | bytes 4194304 | tf_op jit(solution)/shard_map/pallas_call | solution.py:198
  18.0 1.3 %copy.5 = f32[32,128]{1,0:T(8,128)} copy(f32[32,128]{1,0:T(8,128)} %shard_map.37) | data formatting | bytes 32768
where the time goes:
time: 19.6 us; the launch traced here: 19.3 us
  Pallas kernels  18 us (92%)
  local copies, waits for them, and re-layouts  1.32 us (7%)
    pallas_call x1, Pallas kernels, body(): pl.pallas_call(functools.partial(kernel, hi_count, lo_count), out_shape=j...  18 us
    unnamed x1, local copies, waits for them, and re-layouts  1.32 us

commit v1 on v0

--- a/solution.py
+++ b/solution.py
@@ -197,7 +197,7 @@
     chunk = (depth, plane * share, width)
     return pl.pallas_call(
         functools.partial(kernel, hi_count, lo_count),
-        out_shape=jax.ShapeDtypeStruct((share, width), f32),
+        out_shape=pltpu.VMEM((share, width), f32),
         in_specs=[pl.BlockSpec(memory_space=pltpu.HBM)] * 4,
         out_specs=vmem,
         scratch_shapes=[

time: 19.6 us -> 18.2 us (0.929)
  local copies, waits for them, and re-layouts: 1.32 us -> 0.61 us
  Pallas kernels: 18 us -> 17.4 us
    unnamed x1, local copies, waits for them, and re-layouts: 1.32 us -> 0.61 us
    pallas_call x1, Pallas kernels: 18 us -> 17.4 us  [body(): pl.pallas_call(functools.partial(kernel, hi_count, lo_count), out_shape=p...]
where the time goes in v1:
time: 18.2 us; the launch traced here: 18 us
  Pallas kernels  17.4 us (96%)
  local copies, waits for them, and re-layouts  0.61 us (3%)
    pallas_call x1, Pallas kernels, body(): pl.pallas_call(functools.partial(kernel, hi_count, lo_count), out_shape=p...  17.4 us
    unnamed x1, local copies, waits for them, and re-layouts  0.61 us

profile of v1, /device:TPU:0, one launch (start us, length us, event | category | flops | bytes accessed | tf_op | source)
XLA Modules:
  0.0 18.0 jit_solution(12674670354888648588)
XLA Ops:
  0.0 17.4 %shard_map.37 = f32[32,128]{1,0:T(8,128)S(1)} custom-call(f32[8192,128]{1,0:T(8,128)} %panel_hbm.1, f32[64,128]{1,0:T(8,128)} %bitcast.2, s32[1024]{0:T(1024)} %rows_hbm.1, s32[8,128]{1,0:T(8,128)} %bitcast.3), custom_call_target="tpu_custom_call" | custom-call | flops 1073741824 | bytes 4194304 | tf_op jit(solution)/shard_map/pallas_call | solution.py:198
  17.4 0.6 %copy.5 = f32[32,128]{1,0:T(8,128)} copy(f32[32,128]{1,0:T(8,128)S(1)} %shard_map.37) | data formatting | bytes 32768

commit v2 on v1

--- a/solution.py
+++ b/solution.py
@@ -12,6 +12,8 @@
 LOW = 256
 LANES = 128
 TILE = 8
+FUSED = 8
+CUTS = (0, 2, 5, 8)
 
 
 def parity_sign(bits):
@@ -23,11 +25,11 @@
 
 
 def kernel(hi_count, lo_count, panel_hbm, signs_hbm, rows_hbm, picks_hbm, out_ref,
-           panel, signs_ref, rows_ref, picks_ref, field, had, sgn, terms, mine, got_a, got_b, got_c, last,
+           panel, signs_ref, rows_ref, picks_ref, field, had, wide, weights_ref, sgn, terms, mine, got_a, got_b, got_c, last,
            load_sem, small_sem, send_a, recv_a, send_b, recv_b, send_c, recv_c):
     count = panel.shape[0]
-    blocks = count // LOW
     share = out_ref.shape[0]
+    kept = rows_ref.shape[0]
     total = count * hi_count * lo_count
     side = 2 ** ((lo_count.bit_length() - 1) // 2)
     depth = lo_count // side
@@ -46,7 +48,8 @@
     peers_depth = [place(core, level ^ r, spot) for r in range(depth)]
 
     loads = load_sem.shape[0]
-    rows_load = count // loads
+    groups = count // LANES
+    cuts = [c * groups // CUTS[-1] for c in CUTS]
     small = [pltpu.make_async_copy(signs_hbm, signs_ref, small_sem.at[0]),
              pltpu.make_async_copy(picks_hbm, picks_ref, small_sem.at[1]),
              pltpu.make_async_copy(rows_hbm, rows_ref, small_sem.at[2])]
@@ -54,7 +57,7 @@
         copy.start()
 
     def load(i):
-        part = pl.ds(i * rows_load, rows_load)
+        part = pl.ds(cuts[i] * LANES, (cuts[i + 1] - cuts[i]) * LANES)
         return pltpu.make_async_copy(panel_hbm.at[part], panel.at[part], load_sem.at[i])
 
     for i in range(loads):
@@ -65,48 +68,89 @@
     for device in greet:
         pl.semaphore_signal(barrier, inc=1, device_id=device, device_id_type=MESH)
 
-    left = lax.broadcasted_iota(jnp.int32, (LOW, LOW), 0)
-    right = lax.broadcasted_iota(jnp.int32, (LOW, LOW), 1)
-    had[...] = parity_sign(left & right).astype(jnp.bfloat16)
-
-    for copy in small:
-        copy.wait()
-
-    weight = parity_sign((picks_ref[...] // count) & me) * (1.0 / math.sqrt(total))
-    for g in range(weight.shape[0]):
-        sgn[pl.ds(g * LANES, LANES), :] = jnp.broadcast_to(weight[g:g + 1, :], (LANES, LANES)).T
-
-    @pl.loop(0, loads)
-    def _(i):
-        load(i).wait()
-        for step in range(blocks // loads):
-            a = i * (blocks // loads) + step
-            parts = []
-            for h in range(LOW // LANES):
-                line = signs_ref[pl.ds(a * (LOW // LANES) + h, 1), :]
-                wide = jnp.broadcast_to(line, (LANES, LANES)).T
-                parts.append(panel[pl.ds(a * LOW + h * LANES, LANES), :] * wide)
-            block = jnp.concatenate(parts, axis=0)
-            big = block.astype(jnp.bfloat16)
-            small = (block - big.astype(jnp.float32)).astype(jnp.bfloat16)
-            both = jnp.concatenate([big, small], axis=1)
-            done = jnp.dot(had[...], both, preferred_element_type=jnp.float32)
-            field[pl.ds(a * LOW, LOW), :] = done[:, :LANES] + done[:, LANES:]
-
-    @pl.loop(0, LOW // TILE)
-    def _(p):
-        parts = [field[pl.ds(b * LOW + p * TILE, TILE), :] for b in range(blocks)]
-        half = 1
-        while half < blocks:
-            for b in range(blocks):
-                if not b & half:
-                    x, y = parts[b], parts[b + half]
-                    parts[b], parts[b + half] = x + y, x - y
-            half *= 2
-        for b in range(blocks):
-            field[pl.ds(b * LOW + p * TILE, TILE), :] = parts[b]
-
-    pl.semaphore_wait(barrier, len(greet))
+    left = lax.broadcasted_iota(jnp.int32, (LANES, 2 * LANES), 0)
+    right = lax.broadcasted_iota(jnp.int32, (LANES, 2 * LANES), 1)
+    had[...] = parity_sign(left & right & (LANES - 1)).astype(jnp.bfloat16)
+
+    with jax.named_scope("small_waits"):
+        for copy in small:
+            copy.wait()
+
+    ahead = 16
+    more = 12
+
+    def turn(line):
+        return jnp.broadcast_to(line, (LANES, LANES)).T
+
+    def factor(a):
+        return turn(signs_ref[pl.ds(a, 1), :])
+
+    with jax.named_scope("early_factors"):
+        for a in range(ahead):
+            wide[pl.ds(a * LANES, LANES), :] = factor(a)
+
+    ready = ahead
+    for i in range(loads):
+        with jax.named_scope("load_wait"):
+            load(i).wait()
+        with jax.named_scope("products"):
+            stop = cuts[i + 1]
+            later = stop + more if i + 1 < loads else stop
+            held = []
+            extra = list(range(max(ready, stop), later))
+            for pair in range(cuts[i] // 2, stop // 2):
+                big, rest = [], []
+                for q in range(2):
+                    a = 2 * pair + q
+                    rows = pl.ds(a * LANES, LANES)
+                    by = wide[rows, :] if a < ready else factor(a)
+                    block = panel[rows, :] * by
+                    big.append(block.astype(jnp.bfloat16))
+                    rest.append((block - big[q].astype(jnp.float32)).astype(jnp.bfloat16))
+                both = jnp.concatenate(
+                    [jnp.concatenate(big, axis=1), jnp.concatenate(rest, axis=1)], axis=0)
+                done = jnp.dot(had[...], both, preferred_element_type=jnp.float32)
+                x, y = done[:, :LANES], done[:, LANES:]
+                two = [x + y, x - y]
+                held.append(two)
+                while len(held) > 1 and len(held[-1]) == len(held[-2]):
+                    y, x = held.pop(), held.pop()
+                    held.append([u + v for u, v in zip(x, y)] + [u - v for u, v in zip(x, y)])
+                if len(held[0]) == FUSED:
+                    for k, v in enumerate(held.pop()):
+                        field[pl.ds((2 * pair + 2 - FUSED + k) * LANES, LANES), :] = v
+                if extra and pair % 2 == 0:
+                    for a in [extra.pop(0) for _ in range(min(2, len(extra)))]:
+                        wide[pl.ds(a * LANES, LANES), :] = factor(a)
+            for a in extra:
+                wide[pl.ds(a * LANES, LANES), :] = factor(a)
+            ready = later
+
+    with jax.named_scope("butterflies"):
+        steps = groups // FUSED
+        tiles = FUSED * LANES // TILE
+        lines = kept // LANES
+        weights_ref[...] = parity_sign((picks_ref[...] // count) & me) * (1.0 / math.sqrt(total))
+
+        @pl.loop(0, lines)
+        def _(g):
+            sgn[pl.ds(g * LANES, LANES), :] = turn(weights_ref[pl.ds(g, 1), :])
+            for t in range(tiles // lines):
+                p = g * (tiles // lines) + t
+                rows = [pl.ds(b * FUSED * LANES + p * TILE, TILE) for b in range(steps)]
+                parts = [field[r, :] for r in rows]
+                half = 1
+                while half < steps:
+                    for b in range(steps):
+                        if not b & half:
+                            x, y = parts[b], parts[b + half]
+                            parts[b], parts[b + half] = x + y, x - y
+                    half *= 2
+                for b in range(steps):
+                    panel[rows[b], :] = parts[b]
+
+    with jax.named_scope("barw"):
+        pl.semaphore_wait(barrier, len(greet))
 
     def gather(dst, core_to, level_to):
         @pl.loop(0, plane)
@@ -115,7 +159,7 @@
             start = (hi_to * lo_count + lo_to) * share
             for s in range(share):
                 row = rows_ref[start + s] & (count - 1)
-                dst[pl.ds(j * share + s, 1), :] = field[pl.ds(row, 1), :]
+                dst[pl.ds(j * share + s, 1), :] = panel[pl.ds(row, 1), :]
             part = pl.ds(j * share, share)
             dst[part, :] = dst[part, :] * sgn[pl.ds(start, share), :]
 
@@ -128,15 +172,18 @@
     sent_a, sent_b = {}, {}
 
     def send_pair(c):
-        gather(terms.at[c], 1 - core, c)
+        with jax.named_scope("gath1"):
+            gather(terms.at[c], 1 - core, c)
         sent_a[c] = remote(terms.at[c], got_a.at[c], send_a.at[c], recv_a.at[c], partner)
         sent_a[c].start()
         if c:
             send_plane(c - 1)
-        gather(mine.at[c], core, c)
+        with jax.named_scope("gath2"):
+            gather(mine.at[c], core, c)
 
     def send_plane(c):
-        sent_a[c].wait_recv()
+        with jax.named_scope("waita"):
+            sent_a[c].wait_recv()
         for j in list(range(1, plane)) + [0]:
             part = pl.ds(j * share, share)
             mine[c, part, :] = mine[c, part, :] + got_a[c, part, :]
@@ -152,7 +199,8 @@
     def send_level(c):
         rows = mine[c, pl.ds(0, share), :]
         for j in range(1, plane):
-            sent_b[c, j].wait_recv()
+            with jax.named_scope("waitb"):
+                sent_b[c, j].wait_recv()
             rows = rows + got_b[c, pl.ds(j * share, share), :]
         last[c] = rows
 
@@ -168,7 +216,8 @@
     result = last[level]
     for r in range(1, depth):
         other = level ^ r
-        remote(last.at[other], got_c.at[other], send_c.at[other], recv_c.at[other],
+        with jax.named_scope("waitc"):
+            remote(last.at[other], got_c.at[other], send_c.at[other], recv_c.at[other],
                place(core, other, spot)).wait_recv()
         result = result + got_c[other]
     out_ref[...] = result
@@ -190,7 +239,7 @@
     side = 2 ** ((lo_count.bit_length() - 1) // 2)
     depth = lo_count // side
     plane = (hi_count // 2) * side
-    loads = 2
+    loads = len(CUTS) - 1
     vmem = pl.BlockSpec(memory_space=pltpu.VMEM)
     dma = pltpu.SemaphoreType.DMA
     f32 = jnp.float32
@@ -206,7 +255,9 @@
             pltpu.SMEM((kept,), jnp.int32),
             pltpu.VMEM((kept // LANES, LANES), jnp.int32),
             pltpu.VMEM((count, width), f32),
-            pltpu.VMEM((LOW, LOW), jnp.bfloat16),
+            pltpu.VMEM((LANES, 2 * LANES), jnp.bfloat16),
+            pltpu.VMEM((count, width), f32),
+            pltpu.VMEM((kept // LANES, LANES), f32),
             pltpu.VMEM((kept, width), f32),
             pltpu.VMEM(chunk, f32),
             pltpu.VMEM(chunk, f32),

time: 18.2 us -> 17.4 us (0.956)
  Pallas kernels: 17.4 us -> 16.7 us
    pallas_call x1, Pallas kernels: 17.4 us -> 16.7 us  [body(): pl.pallas_call(functools.partial(kernel, hi_count, lo_count), out_shape=p...]
where the time goes in v2:
time: 17.4 us; the launch traced here: 17.3 us
  Pallas kernels  16.7 us (96%)
  local copies, waits for them, and re-layouts  0.61 us (4%)
    pallas_call x1, Pallas kernels, body(): pl.pallas_call(functools.partial(kernel, hi_count, lo_count), out_shape=p...  16.7 us
    unnamed x1, local copies, waits for them, and re-layouts  0.61 us

profile of v2, /device:TPU:0, one launch (start us, length us, event | category | flops | bytes accessed | tf_op | source)
XLA Modules:
  0.0 17.3 jit_solution(3736256893417870746)
XLA Ops:
  0.0 16.7 %shard_map.37 = f32[32,128]{1,0:T(8,128)S(1)} custom-call(f32[8192,128]{1,0:T(8,128)} %panel_hbm.1, f32[64,128]{1,0:T(8,128)} %bitcast.2, s32[1024]{0:T(1024)} %rows_hbm.1, s32[8,128]{1,0:T(8,128)} %bitcast.3), custom_call_target="tpu_custom_call" | custom-call | flops 1073741824 | bytes 4194304 | tf_op jit(solution)/shard_map/pallas_call | solution.py:247
  16.7 0.6 %copy.5 = f32[32,128]{1,0:T(8,128)} copy(f32[32,128]{1,0:T(8,128)S(1)} %shard_map.37) | data formatting | bytes 32768

commit v3 on v2

--- a/solution.py
+++ b/solution.py
@@ -25,8 +25,10 @@
 
 
 def kernel(hi_count, lo_count, panel_hbm, signs_hbm, rows_hbm, picks_hbm, out_ref,
-           panel, signs_ref, rows_ref, picks_ref, field, had, wide, weights_ref, sgn, terms, mine, got_a, got_b, got_c, last,
-           load_sem, small_sem, send_a, recv_a, send_b, recv_b, send_c, recv_c):
+           panel, signs_ref, rows_ref, picks_ref, field, had, wide, sgn, terms, mine, got_a, got_b, got_c, last,
+           first, got_first, head, got_head,
+           load_sem, small_sem, send_a, recv_a, send_b, recv_b, send_c, recv_c,
+           send_f, recv_f, send_h, recv_h):
     count = panel.shape[0]
     share = out_ref.shape[0]
     kept = rows_ref.shape[0]
@@ -65,6 +67,7 @@
 
     barrier = pltpu.get_barrier_semaphore()
     greet = [partner] + peers_plane[1:] + peers_depth[1:]
+    greet += [place(1 - core, level, spot ^ j) for j in range(1, plane)]
     for device in greet:
         pl.semaphore_signal(barrier, inc=1, device_id=device, device_id_type=MESH)
 
@@ -76,8 +79,8 @@
         for copy in small:
             copy.wait()
 
-    ahead = 16
-    more = 12
+    ahead = 8
+    more = 8
 
     def turn(line):
         return jnp.broadcast_to(line, (LANES, LANES)).T
@@ -97,6 +100,10 @@
             stop = cuts[i + 1]
             later = stop + more if i + 1 < loads else stop
             held = []
+            lines = []
+            if i == loads - 1:
+                weight = parity_sign((picks_ref[...] // count) & me) * (1.0 / math.sqrt(total))
+                lines = list(range(kept // LANES))
             extra = list(range(max(ready, stop), later))
             for pair in range(cuts[i] // 2, stop // 2):
                 big, rest = [], []
@@ -119,9 +126,14 @@
                 if len(held[0]) == FUSED:
                     for k, v in enumerate(held.pop()):
                         field[pl.ds((2 * pair + 2 - FUSED + k) * LANES, LANES), :] = v
+                if lines:
+                    g = lines.pop(0)
+                    sgn[pl.ds(g * LANES, LANES), :] = turn(weight[g:g + 1, :])
                 if extra and pair % 2 == 0:
                     for a in [extra.pop(0) for _ in range(min(2, len(extra)))]:
                         wide[pl.ds(a * LANES, LANES), :] = factor(a)
+            for g in lines:
+                sgn[pl.ds(g * LANES, LANES), :] = turn(weight[g:g + 1, :])
             for a in extra:
                 wide[pl.ds(a * LANES, LANES), :] = factor(a)
             ready = later
@@ -129,12 +141,10 @@
     with jax.named_scope("butterflies"):
         steps = groups // FUSED
         tiles = FUSED * LANES // TILE
-        lines = kept // LANES
-        weights_ref[...] = parity_sign((picks_ref[...] // count) & me) * (1.0 / math.sqrt(total))
+        lines = 8
 
         @pl.loop(0, lines)
         def _(g):
-            sgn[pl.ds(g * LANES, LANES), :] = turn(weights_ref[pl.ds(g, 1), :])
             for t in range(tiles // lines):
                 p = g * (tiles // lines) + t
                 rows = [pl.ds(b * FUSED * LANES + p * TILE, TILE) for b in range(steps)]
@@ -149,19 +159,27 @@
                 for b in range(steps):
                     panel[rows[b], :] = parts[b]
 
-    with jax.named_scope("barw"):
+    with jax.named_scope("entry_wait"):
         pl.semaphore_wait(barrier, len(greet))
 
-    def gather(dst, core_to, level_to):
+    def gather(dst, base, core_to, level_to, spot_to):
+        hi_to, lo_to = place(core_to, level_to, spot_to)
+        start = (hi_to * lo_count + lo_to) * share
+        for s in range(share):
+            row = rows_ref[start + s] & (count - 1)
+            dst[pl.ds(base + s, 1), :] = panel[pl.ds(row, 1), :]
+        part = pl.ds(base, share)
+        dst[part, :] = dst[part, :] * sgn[pl.ds(start, share), :]
+
+    def gather_level(dst, core_to, level_to):
         @pl.loop(0, plane)
         def _(j):
-            hi_to, lo_to = place(core_to, level_to, spot ^ j)
-            start = (hi_to * lo_count + lo_to) * share
-            for s in range(share):
-                row = rows_ref[start + s] & (count - 1)
-                dst[pl.ds(j * share + s, 1), :] = panel[pl.ds(row, 1), :]
-            part = pl.ds(j * share, share)
-            dst[part, :] = dst[part, :] * sgn[pl.ds(start, share), :]
+            if level_to:
+                gather(dst, j * share, core_to, level_to, spot ^ j)
+            else:
+                @pl.when(spot != j)
+                def _():
+                    gather(dst, j * share, core_to, level_to, spot ^ j)
 
     def remote(src, dst, send, recv, device):
         return pltpu.make_async_remote_copy(
@@ -169,66 +187,129 @@
             device_id=device, device_id_type=MESH)
 
     levels = range(depth)
-    sent_a, sent_b = {}, {}
+
+    def to_first(k):
+        return remote(first.at[k], got_first.at[spot * 2 + core], send_f.at[k], recv_f.at[spot * 2 + core],
+                      place(k, level, 0))
+
+    def to_partner(c):
+        return remote(terms.at[c], got_a.at[c], send_a.at[c], recv_a.at[c], partner)
+
+    def to_plane(c, j):
+        part = pl.ds(j * share, share)
+        return remote(mine.at[c, part], got_b.at[c, part], send_b.at[c, j], recv_b.at[c, j], peers_plane[j])
+
+    def to_level(c):
+        return remote(last.at[c], got_c.at[level], send_c.at[c], recv_c.at[level], place(core, c, spot))
+
+    def to_head():
+        return remote(head, got_head.at[level], send_h.at[0], recv_h.at[level], place(core, 0, 0))
+
+    def guarded(condition, action):
+        pl.when(condition)(action)
+
+    def send_first():
+        for k in range(2):
+            gather(first.at[k], 0, k, 0, 0)
+            guarded((spot != 0) | (core != k), lambda k=k: to_first(k).start())
 
     def send_pair(c):
-        with jax.named_scope("gath1"):
-            gather(terms.at[c], 1 - core, c)
-        sent_a[c] = remote(terms.at[c], got_a.at[c], send_a.at[c], recv_a.at[c], partner)
-        sent_a[c].start()
-        if c:
-            send_plane(c - 1)
-        with jax.named_scope("gath2"):
-            gather(mine.at[c], core, c)
+        gather_level(terms.at[c], 1 - core, c)
+        to_partner(c).start()
 
     def send_plane(c):
-        with jax.named_scope("waita"):
-            sent_a[c].wait_recv()
-        for j in list(range(1, plane)) + [0]:
+        gather_level(mine.at[c], core, c)
+        with jax.named_scope("partner_wait"):
+            to_partner(c).wait_recv()
+
+        def part_sum(j):
             part = pl.ds(j * share, share)
             mine[c, part, :] = mine[c, part, :] + got_a[c, part, :]
             if j:
-                sent_b[c, j] = remote(mine.at[c, part], got_b.at[c, part],
-                                      send_b.at[c, j], recv_b.at[c, j], peers_plane[j])
-                sent_b[c, j].start()
-
-    def to_level(c):
-        return remote(last.at[c], got_c.at[level], send_c.at[c], recv_c.at[level],
-                      place(core, c, spot))
+                to_plane(c, j).start()
+
+        for j in list(range(1, plane)) + [0]:
+            if c:
+                part_sum(j)
+            else:
+                guarded(spot != j, lambda j=j: part_sum(j))
+
+    def sum_first():
+        total = first[core]
+        with jax.named_scope("first_wait"):
+            for i in range(2 * plane):
+                def arrived(i=i):
+                    remote(first.at[0], got_first.at[i], send_f.at[0], recv_f.at[i], partner).wait_recv()
+                if i < 2:
+                    guarded(core != i, arrived)
+                else:
+                    arrived()
+        total = total + got_first[1 - core]
+        for i in range(2, 2 * plane):
+            total = total + got_first[i]
+        head[...] = total
+        guarded(level != 0, lambda: to_head().start())
 
     def send_level(c):
         rows = mine[c, pl.ds(0, share), :]
         for j in range(1, plane):
-            with jax.named_scope("waitb"):
-                sent_b[c, j].wait_recv()
+            with jax.named_scope("plane_wait"):
+                to_plane(c, j).wait_recv()
             rows = rows + got_b[c, pl.ds(j * share, share), :]
         last[c] = rows
-
-        @pl.when(level != c)
-        def _():
-            to_level(c).start()
-
+        guarded(level != c, lambda: to_level(c).start())
+
+    with jax.named_scope("first_rows"):
+        send_first()
+    lead = min(3, depth)
+    for c in range(lead):
+        with jax.named_scope("gather_partner"):
+            send_pair(c)
     for c in levels:
-        send_pair(c)
-    send_plane(depth - 1)
+        with jax.named_scope("gather_own"):
+            send_plane(c)
+        if c + lead < depth:
+            send_pair(c + lead)
+
+    guarded(spot == 0, sum_first)
+    guarded(spot != 0, lambda: send_level(0))
+    for c in levels[1:]:
+        send_level(c)
+
+    is_first = (spot == 0) & (level == 0)
+
+    @pl.when(is_first)
+    def _():
+        result = head[...]
+        for other in range(1, depth):
+            with jax.named_scope("head_wait"):
+                remote(head, got_head.at[other], send_h.at[0], recv_h.at[other], partner).wait_recv()
+            result = result + got_head[other]
+        out_ref[...] = result
+
+    @pl.when(jnp.logical_not(is_first))
+    def _():
+        result = last[level]
+        for r in range(1, depth):
+            other = level ^ r
+            with jax.named_scope("level_wait"):
+                remote(last.at[other], got_c.at[other], send_c.at[other], recv_c.at[other],
+                       place(core, other, spot)).wait_recv()
+            result = result + got_c[other]
+        out_ref[...] = result
+
+    for k in range(2):
+        guarded((spot != 0) | (core != k), lambda k=k: to_first(k).wait_send())
+    guarded((spot == 0) & (level != 0), lambda: to_head().wait_send())
     for c in levels:
-        send_level(c)
-    result = last[level]
-    for r in range(1, depth):
-        other = level ^ r
-        with jax.named_scope("waitc"):
-            remote(last.at[other], got_c.at[other], send_c.at[other], recv_c.at[other],
-               place(core, other, spot)).wait_recv()
-        result = result + got_c[other]
-    out_ref[...] = result
-    for c in levels:
-        sent_a[c].wait_send()
+        to_partner(c).wait_send()
         for j in range(1, plane):
-            sent_b[c, j].wait_send()
-
-        @pl.when(level != c)
-        def _():
-            to_level(c).wait_send()
+            if c:
+                to_plane(c, j).wait_send()
+            else:
+                guarded(spot != j, lambda j=j: to_plane(0, j).wait_send())
+        there = level != c
+        guarded(there if c else there & (spot != 0), lambda c=c: to_level(c).wait_send())
 
 
 def body(panel, row_signs, sample_rows):
@@ -257,7 +338,6 @@
             pltpu.VMEM((count, width), f32),
             pltpu.VMEM((LANES, 2 * LANES), jnp.bfloat16),
             pltpu.VMEM((count, width), f32),
-            pltpu.VMEM((kept // LANES, LANES), f32),
             pltpu.VMEM((kept, width), f32),
             pltpu.VMEM(chunk, f32),
             pltpu.VMEM(chunk, f32),
@@ -265,10 +345,16 @@
             pltpu.VMEM(chunk, f32),
             pltpu.VMEM((depth, share, width), f32),
             pltpu.VMEM((depth, share, width), f32),
+            pltpu.VMEM((2, share, width), f32),
+            pltpu.VMEM((2 * plane, share, width), f32),
+            pltpu.VMEM((share, width), f32),
+            pltpu.VMEM((depth, share, width), f32),
             dma((loads,)), dma((3,)),
             dma((depth,)), dma((depth,)),
             dma((depth, plane)), dma((depth, plane)),
             dma((depth,)), dma((depth,)),
+            dma((2,)), dma((2 * plane,)),
+            dma((1,)), dma((depth,)),
         ],
         compiler_params=pltpu.CompilerParams(
             collective_id=0, has_side_effects=True, vmem_limit_bytes=60 * 2**20),

time: 17.4 us -> 16 us (0.920)
  Pallas kernels: 16.7 us -> 15.3 us
    pallas_call x1, Pallas kernels: 16.7 us -> 15.3 us  [body(): pl.pallas_call(functools.partial(kernel, hi_count, lo_count), out_shape=p...]
where the time goes in v3:
time: 16 us; the launch traced here: 15.9 us
  Pallas kernels  15.3 us (96%)
  local copies, waits for them, and re-layouts  0.61 us (4%)
    pallas_call x1, Pallas kernels, body(): pl.pallas_call(functools.partial(kernel, hi_count, lo_count), out_shape=p...  15.3 us
    unnamed x1, local copies, waits for them, and re-layouts  0.61 us

profile of v3, /device:TPU:0, one launch (start us, length us, event | category | flops | bytes accessed | tf_op | source)
XLA Modules:
  0.0 15.9 jit_solution(11097707228292416349)
XLA Ops:
  0.0 15.3 %shard_map.37 = f32[32,128]{1,0:T(8,128)S(1)} custom-call(f32[8192,128]{1,0:T(8,128)} %panel_hbm.1, f32[64,128]{1,0:T(8,128)} %bitcast.2, s32[1024]{0:T(1024)} %rows_hbm.1, s32[8,128]{1,0:T(8,128)} %bitcast.3), custom_call_target="tpu_custom_call" | custom-call | flops 1073741824 | bytes 4194304 | tf_op jit(solution)/shard_map/pallas_call | solution.py:328
  15.3 0.6 %copy.5 = f32[32,128]{1,0:T(8,128)} copy(f32[32,128]{1,0:T(8,128)S(1)} %shard_map.37) | data formatting | bytes 32768

commit v4 on v3

--- a/solution.py
+++ b/solution.py
@@ -68,6 +68,7 @@
     barrier = pltpu.get_barrier_semaphore()
     greet = [partner] + peers_plane[1:] + peers_depth[1:]
     greet += [place(1 - core, level, spot ^ j) for j in range(1, plane)]
+    greet += [place(1 - core, level ^ r, spot) for r in range(1, depth)]
     for device in greet:
         pl.semaphore_signal(barrier, inc=1, device_id=device, device_id_type=MESH)
 
@@ -188,22 +189,30 @@
 
     levels = range(depth)
 
-    def to_first(k):
-        return remote(first.at[k], got_first.at[spot * 2 + core], send_f.at[k], recv_f.at[spot * 2 + core],
-                      place(k, level, 0))
+    reducer = (core == 1) & (spot == 0)
+    slot = (spot * 2 + core) ^ 1
+
+    def to_first():
+        return remote(first, got_first.at[slot], send_f.at[0], recv_f.at[0], place(1, level, 0))
+
+    def to_head(k):
+        return remote(head.at[k], got_head.at[level], send_h.at[0], recv_h.at[0], place(k, 0, 0))
 
     def to_partner(c):
-        return remote(terms.at[c], got_a.at[c], send_a.at[c], recv_a.at[c], partner)
+        return remote(terms.at[c], got_a.at[c], send_a.at[0], recv_a.at[c], partner)
 
     def to_plane(c, j):
         part = pl.ds(j * share, share)
-        return remote(mine.at[c, part], got_b.at[c, part], send_b.at[c, j], recv_b.at[c, j], peers_plane[j])
+        return remote(mine.at[c, part], got_b.at[c, part], send_b.at[min(c, 1)], recv_b.at[c], peers_plane[j])
 
     def to_level(c):
-        return remote(last.at[c], got_c.at[level], send_c.at[c], recv_c.at[level], place(core, c, spot))
-
-    def to_head():
-        return remote(head, got_head.at[level], send_h.at[0], recv_h.at[level], place(core, 0, 0))
+        return remote(last.at[c], got_c.at[level], send_c.at[0], recv_c.at[0], place(core, c, spot))
+
+    def received(ref, recv):
+        remote(ref, ref, send_f.at[0], recv, partner).wait_recv()
+
+    def sent(ref, send):
+        remote(ref, ref, send, recv_f.at[0], partner).wait_send()
 
     def guarded(condition, action):
         pl.when(condition)(action)
@@ -211,7 +220,7 @@
     def send_first():
         for k in range(2):
             gather(first.at[k], 0, k, 0, 0)
-            guarded((spot != 0) | (core != k), lambda k=k: to_first(k).start())
+        guarded(jnp.logical_not(reducer), lambda: to_first().start())
 
     def send_pair(c):
         gather_level(terms.at[c], 1 - core, c)
@@ -235,26 +244,23 @@
                 guarded(spot != j, lambda j=j: part_sum(j))
 
     def sum_first():
-        total = first[core]
         with jax.named_scope("first_wait"):
-            for i in range(2 * plane):
-                def arrived(i=i):
-                    remote(first.at[0], got_first.at[i], send_f.at[0], recv_f.at[i], partner).wait_recv()
-                if i < 2:
-                    guarded(core != i, arrived)
-                else:
-                    arrived()
-        total = total + got_first[1 - core]
-        for i in range(2, 2 * plane):
-            total = total + got_first[i]
-        head[...] = total
-        guarded(level != 0, lambda: to_head().start())
+            received(got_first.at[pl.ds(1, 2 * plane - 1)], recv_f.at[0])
+        for k in range(2):
+            total = first[k]
+            for i in range(1, 2 * plane):
+                total = total + got_first[i, k]
+            head[k] = total
+            if k:
+                guarded(level != 0, lambda: to_head(1).start())
+            else:
+                to_head(0).start()
 
     def send_level(c):
+        with jax.named_scope("plane_wait"):
+            received(got_b.at[c, pl.ds(share, (plane - 1) * share)], recv_b.at[c])
         rows = mine[c, pl.ds(0, share), :]
         for j in range(1, plane):
-            with jax.named_scope("plane_wait"):
-                to_plane(c, j).wait_recv()
             rows = rows + got_b[c, pl.ds(j * share, share), :]
         last[c] = rows
         guarded(level != c, lambda: to_level(c).start())
@@ -271,45 +277,51 @@
         if c + lead < depth:
             send_pair(c + lead)
 
-    guarded(spot == 0, sum_first)
+    guarded(reducer, sum_first)
     guarded(spot != 0, lambda: send_level(0))
     for c in levels[1:]:
         send_level(c)
 
     is_first = (spot == 0) & (level == 0)
-
-    @pl.when(is_first)
+    others = pl.ds(1, depth - 1)
+
+    @pl.when(is_first & (core == 0))
     def _():
-        result = head[...]
+        with jax.named_scope("head_wait"):
+            received(got_head, recv_h.at[0])
+        result = got_head[0]
         for other in range(1, depth):
-            with jax.named_scope("head_wait"):
-                remote(head, got_head.at[other], send_h.at[0], recv_h.at[other], partner).wait_recv()
             result = result + got_head[other]
         out_ref[...] = result
 
+    @pl.when(is_first & (core == 1))
+    def _():
+        with jax.named_scope("head_wait"):
+            received(got_head.at[others], recv_h.at[0])
+        result = head[1]
+        for other in range(1, depth):
+            result = result + got_head[other]
+        out_ref[...] = result
+
     @pl.when(jnp.logical_not(is_first))
     def _():
+        with jax.named_scope("level_wait"):
+            received(got_c.at[others], recv_c.at[0])
         result = last[level]
         for r in range(1, depth):
-            other = level ^ r
-            with jax.named_scope("level_wait"):
-                remote(last.at[other], got_c.at[other], send_c.at[other], recv_c.at[other],
-                       place(core, other, spot)).wait_recv()
-            result = result + got_c[other]
+            result = result + got_c[level ^ r]
         out_ref[...] = result
 
-    for k in range(2):
-        guarded((spot != 0) | (core != k), lambda k=k: to_first(k).wait_send())
-    guarded((spot == 0) & (level != 0), lambda: to_head().wait_send())
-    for c in levels:
-        to_partner(c).wait_send()
-        for j in range(1, plane):
-            if c:
-                to_plane(c, j).wait_send()
-            else:
-                guarded(spot != j, lambda j=j: to_plane(0, j).wait_send())
-        there = level != c
-        guarded(there if c else there & (spot != 0), lambda c=c: to_level(c).wait_send())
+    guarded(jnp.logical_not(reducer), lambda: to_first().wait_send())
+    guarded(reducer & (level != 0), lambda: sent(head, send_h.at[0]))
+    guarded(reducer & (level == 0), lambda: to_head(0).wait_send())
+    sent(terms, send_a.at[0])
+    sent(mine.at[others, pl.ds(share, (plane - 1) * share)], send_b.at[1])
+    guarded(spot == 0, lambda: sent(mine.at[0, pl.ds(share, (plane - 1) * share)], send_b.at[0]))
+    guarded(spot != 0, lambda: sent(mine.at[0, pl.ds(share, (plane - 2) * share)], send_b.at[0]))
+    fewer = (spot == 0) & (level != 0)
+    guarded(fewer, lambda: sent(last.at[pl.ds(0, depth - 2)], send_c.at[0]))
+    guarded(jnp.logical_not(fewer), lambda: sent(last.at[pl.ds(0, depth - 1)], send_c.at[0]))
 
 
 def body(panel, row_signs, sample_rows):
@@ -346,15 +358,15 @@
             pltpu.VMEM((depth, share, width), f32),
             pltpu.VMEM((depth, share, width), f32),
             pltpu.VMEM((2, share, width), f32),
-            pltpu.VMEM((2 * plane, share, width), f32),
-            pltpu.VMEM((share, width), f32),
+            pltpu.VMEM((2 * plane, 2, share, width), f32),
+            pltpu.VMEM((2, share, width), f32),
             pltpu.VMEM((depth, share, width), f32),
             dma((loads,)), dma((3,)),
-            dma((depth,)), dma((depth,)),
-            dma((depth, plane)), dma((depth, plane)),
-            dma((depth,)), dma((depth,)),
-            dma((2,)), dma((2 * plane,)),
             dma((1,)), dma((depth,)),
+            dma((2,)), dma((depth,)),
+            dma((1,)), dma((1,)),
+            dma((1,)), dma((1,)),
+            dma((1,)), dma((1,)),
         ],
         compiler_params=pltpu.CompilerParams(
             collective_id=0, has_side_effects=True, vmem_limit_bytes=60 * 2**20),

time: 16 us -> 15.1 us (0.944); the launches traced: 15.9 us -> 14.8 us
  Pallas kernels: 15.3 us -> 14.2 us
    pallas_call x1, Pallas kernels: 15.3 us -> 14.2 us  [body(): pl.pallas_call(functools.partial(kernel, hi_count, lo_count), out_shape=p...]
where the time goes in v4:
time: 15.1 us; the launch traced here: 14.8 us
  Pallas kernels  14.2 us (94%)
  local copies, waits for them, and re-layouts  0.61 us (4%)
    pallas_call x1, Pallas kernels, body(): pl.pallas_call(functools.partial(kernel, hi_count, lo_count), out_shape=p...  14.2 us
    unnamed x1, local copies, waits for them, and re-layouts  0.61 us

profile of v4, /device:TPU:0, one launch (start us, length us, event | category | flops | bytes accessed | tf_op | source)
XLA Modules:
  0.0 14.8 jit_solution(4805374896447200121)
XLA Ops:
  0.0 14.2 %shard_map.37 = f32[32,128]{1,0:T(8,128)S(1)} custom-call(f32[8192,128]{1,0:T(8,128)} %panel_hbm.1, f32[64,128]{1,0:T(8,128)} %bitcast.2, s32[1024]{0:T(1024)} %rows_hbm.1, s32[8,128]{1,0:T(8,128)} %bitcast.3), custom_call_target="tpu_custom_call" | custom-call | flops 1073741824 | bytes 4194304 | tf_op jit(solution)/shard_map/pallas_call | solution.py:340
  14.2 0.6 %copy.5 = f32[32,128]{1,0:T(8,128)} copy(f32[32,128]{1,0:T(8,128)S(1)} %shard_map.37) | data formatting | bytes 32768

commit v5 on v4

--- a/solution.py
+++ b/solution.py
@@ -192,8 +192,8 @@
     reducer = (core == 1) & (spot == 0)
     slot = (spot * 2 + core) ^ 1
 
-    def to_first():
-        return remote(first, got_first.at[slot], send_f.at[0], recv_f.at[0], place(1, level, 0))
+    def to_first(k):
+        return remote(first.at[k], got_first.at[k, slot], send_f.at[0], recv_f.at[k], place(1, level, 0))
 
     def to_head(k):
         return remote(head.at[k], got_head.at[level], send_h.at[0], recv_h.at[0], place(k, 0, 0))
@@ -203,10 +203,11 @@
 
     def to_plane(c, j):
         part = pl.ds(j * share, share)
-        return remote(mine.at[c, part], got_b.at[c, part], send_b.at[min(c, 1)], recv_b.at[c], peers_plane[j])
-
-    def to_level(c):
-        return remote(last.at[c], got_c.at[level], send_c.at[0], recv_c.at[0], place(core, c, spot))
+        return remote(mine.at[c, part], got_b.at[core, c, part], send_b.at[min(c, 1)], recv_b.at[core, c],
+                      place(1, level, spot ^ j))
+
+    def to_level(k, c):
+        return remote(last.at[k, c], got_c.at[level], send_c.at[k], recv_c.at[0], place(k, c, spot))
 
     def received(ref, recv):
         remote(ref, ref, send_f.at[0], recv, partner).wait_recv()
@@ -220,7 +221,7 @@
     def send_first():
         for k in range(2):
             gather(first.at[k], 0, k, 0, 0)
-        guarded(jnp.logical_not(reducer), lambda: to_first().start())
+            guarded(jnp.logical_not(reducer), lambda k=k: to_first(k).start())
 
     def send_pair(c):
         gather_level(terms.at[c], 1 - core, c)
@@ -236,6 +237,8 @@
             mine[c, part, :] = mine[c, part, :] + got_a[c, part, :]
             if j:
                 to_plane(c, j).start()
+            else:
+                guarded(core == 0, lambda: to_plane(c, 0).start())
 
         for j in list(range(1, plane)) + [0]:
             if c:
@@ -244,12 +247,12 @@
                 guarded(spot != j, lambda j=j: part_sum(j))
 
     def sum_first():
-        with jax.named_scope("first_wait"):
-            received(got_first.at[pl.ds(1, 2 * plane - 1)], recv_f.at[0])
         for k in range(2):
+            with jax.named_scope("first_wait"):
+                received(got_first.at[k, pl.ds(1, 2 * plane - 1)], recv_f.at[k])
             total = first[k]
             for i in range(1, 2 * plane):
-                total = total + got_first[i, k]
+                total = total + got_first[k, i]
             head[k] = total
             if k:
                 guarded(level != 0, lambda: to_head(1).start())
@@ -258,12 +261,19 @@
 
     def send_level(c):
         with jax.named_scope("plane_wait"):
-            received(got_b.at[c, pl.ds(share, (plane - 1) * share)], recv_b.at[c])
+            received(got_b.at[1, c, pl.ds(share, (plane - 1) * share)], recv_b.at[1, c])
         rows = mine[c, pl.ds(0, share), :]
         for j in range(1, plane):
-            rows = rows + got_b[c, pl.ds(j * share, share), :]
-        last[c] = rows
-        guarded(level != c, lambda: to_level(c).start())
+            rows = rows + got_b[1, c, pl.ds(j * share, share), :]
+        last[1, c] = rows
+        guarded(level != c, lambda: to_level(1, c).start())
+        with jax.named_scope("plane_wait_other"):
+            received(got_b.at[0, c], recv_b.at[0, c])
+        rows = got_b[0, c, pl.ds(0, share), :]
+        for j in range(1, plane):
+            rows = rows + got_b[0, c, pl.ds(j * share, share), :]
+        last[0, c] = rows
+        to_level(0, c).start()
 
     with jax.named_scope("first_rows"):
         send_first()
@@ -278,9 +288,12 @@
             send_pair(c + lead)
 
     guarded(reducer, sum_first)
-    guarded(spot != 0, lambda: send_level(0))
-    for c in levels[1:]:
-        send_level(c)
+    guarded((core == 1) & (spot != 0), lambda: send_level(0))
+
+    @pl.when(core == 1)
+    def _():
+        for c in levels[1:]:
+            send_level(c)
 
     is_first = (spot == 0) & (level == 0)
     others = pl.ds(1, depth - 1)
@@ -303,25 +316,44 @@
             result = result + got_head[other]
         out_ref[...] = result
 
-    @pl.when(jnp.logical_not(is_first))
+    @pl.when(jnp.logical_not(is_first) & (core == 0))
+    def _():
+        with jax.named_scope("level_wait"):
+            received(got_c, recv_c.at[0])
+        result = got_c[0]
+        for other in range(1, depth):
+            result = result + got_c[other]
+        out_ref[...] = result
+
+    @pl.when(jnp.logical_not(is_first) & (core == 1))
     def _():
         with jax.named_scope("level_wait"):
             received(got_c.at[others], recv_c.at[0])
-        result = last[level]
+        result = last[1, level]
         for r in range(1, depth):
             result = result + got_c[level ^ r]
         out_ref[...] = result
 
-    guarded(jnp.logical_not(reducer), lambda: to_first().wait_send())
+    guarded(jnp.logical_not(reducer), lambda: sent(first, send_f.at[0]))
     guarded(reducer & (level != 0), lambda: sent(head, send_h.at[0]))
     guarded(reducer & (level == 0), lambda: to_head(0).wait_send())
     sent(terms, send_a.at[0])
-    sent(mine.at[others, pl.ds(share, (plane - 1) * share)], send_b.at[1])
-    guarded(spot == 0, lambda: sent(mine.at[0, pl.ds(share, (plane - 1) * share)], send_b.at[0]))
-    guarded(spot != 0, lambda: sent(mine.at[0, pl.ds(share, (plane - 2) * share)], send_b.at[0]))
-    fewer = (spot == 0) & (level != 0)
-    guarded(fewer, lambda: sent(last.at[pl.ds(0, depth - 2)], send_c.at[0]))
-    guarded(jnp.logical_not(fewer), lambda: sent(last.at[pl.ds(0, depth - 1)], send_c.at[0]))
+
+    @pl.when(core == 0)
+    def _():
+        sent(mine.at[others], send_b.at[1])
+        sent(mine.at[0, pl.ds(0, (plane - 1) * share)], send_b.at[0])
+
+    @pl.when(core == 1)
+    def _():
+        sent(mine.at[others, pl.ds(share, (plane - 1) * share)], send_b.at[1])
+        guarded(spot == 0, lambda: sent(mine.at[0, pl.ds(0, (plane - 1) * share)], send_b.at[0]))
+        guarded(spot != 0, lambda: sent(mine.at[0, pl.ds(0, (plane - 2) * share)], send_b.at[0]))
+        guarded(spot == 0, lambda: sent(last.at[0, others], send_c.at[0]))
+        guarded(spot != 0, lambda: sent(last.at[0], send_c.at[0]))
+        fewer = (spot == 0) & (level != 0)
+        guarded(fewer, lambda: sent(last.at[1, pl.ds(0, depth - 2)], send_c.at[1]))
+        guarded(jnp.logical_not(fewer), lambda: sent(last.at[1, others], send_c.at[1]))
 
 
 def body(panel, row_signs, sample_rows):
@@ -354,18 +386,18 @@
             pltpu.VMEM(chunk, f32),
             pltpu.VMEM(chunk, f32),
             pltpu.VMEM(chunk, f32),
-            pltpu.VMEM(chunk, f32),
+            pltpu.VMEM((2,) + chunk, f32),
             pltpu.VMEM((depth, share, width), f32),
-            pltpu.VMEM((depth, share, width), f32),
+            pltpu.VMEM((2, depth, share, width), f32),
             pltpu.VMEM((2, share, width), f32),
-            pltpu.VMEM((2 * plane, 2, share, width), f32),
+            pltpu.VMEM((2, 2 * plane, share, width), f32),
             pltpu.VMEM((2, share, width), f32),
             pltpu.VMEM((depth, share, width), f32),
             dma((loads,)), dma((3,)),
             dma((1,)), dma((depth,)),
-            dma((2,)), dma((depth,)),
-            dma((1,)), dma((1,)),
-            dma((1,)), dma((1,)),
+            dma((2,)), dma((2, depth)),
+            dma((2,)), dma((1,)),
+            dma((1,)), dma((2,)),
             dma((1,)), dma((1,)),
         ],
         compiler_params=pltpu.CompilerParams(

time: 15.1 us -> 14.8 us (0.980)
  Pallas kernels: 14.2 us -> 14 us
    pallas_call x1, Pallas kernels: 14.2 us -> 14 us  [body(): pl.pallas_call(functools.partial(kernel, hi_count, lo_count), out_shape=p...]
where the time goes in v5:
time: 14.8 us; the launch traced here: 14.6 us
  Pallas kernels  14 us (95%)
  local copies, waits for them, and re-layouts  0.61 us (4%)
    pallas_call x1, Pallas kernels, body(): pl.pallas_call(functools.partial(kernel, hi_count, lo_count), out_shape=p...  14 us
    unnamed x1, local copies, waits for them, and re-layouts  0.61 us

profile of v5, /device:TPU:0, one launch (start us, length us, event | category | flops | bytes accessed | tf_op | source)
XLA Modules:
  0.0 14.6 jit_solution(16451814064785408156)
XLA Ops:
  0.0 14.0 %shard_map.37 = f32[32,128]{1,0:T(8,128)S(1)} custom-call(f32[8192,128]{1,0:T(8,128)} %panel_hbm.1, f32[64,128]{1,0:T(8,128)} %bitcast.2, s32[1024]{0:T(1024)} %rows_hbm.1, s32[8,128]{1,0:T(8,128)} %bitcast.3), custom_call_target="tpu_custom_call" | custom-call | flops 1073741824 | bytes 4194304 | tf_op jit(solution)/shard_map/pallas_call | solution.py:372
  14.0 0.6 %copy.5 = f32[32,128]{1,0:T(8,128)} copy(f32[32,128]{1,0:T(8,128)S(1)} %shard_map.37) | data formatting | bytes 32768

commit v6 on v5

--- a/solution.py
+++ b/solution.py
@@ -26,9 +26,9 @@
 
 def kernel(hi_count, lo_count, panel_hbm, signs_hbm, rows_hbm, picks_hbm, out_ref,
            panel, signs_ref, rows_ref, picks_ref, field, had, wide, sgn, terms, mine, got_a, got_b, got_c, last,
-           first, got_first, head, got_head,
+           first, got_first, head, got_head, got_far,
            load_sem, small_sem, send_a, recv_a, send_b, recv_b, send_c, recv_c,
-           send_f, recv_f, send_h, recv_h):
+           send_f, recv_f, send_h, recv_h, recv_d):
     count = panel.shape[0]
     share = out_ref.shape[0]
     kept = rows_ref.shape[0]
@@ -62,26 +62,38 @@
         part = pl.ds(cuts[i] * LANES, (cuts[i + 1] - cuts[i]) * LANES)
         return pltpu.make_async_copy(panel_hbm.at[part], panel.at[part], load_sem.at[i])
 
-    for i in range(loads):
-        load(i).start()
+    load(0).start()
 
     barrier = pltpu.get_barrier_semaphore()
-    greet = [partner] + peers_plane[1:] + peers_depth[1:]
-    greet += [place(1 - core, level, spot ^ j) for j in range(1, plane)]
-    greet += [place(1 - core, level ^ r, spot) for r in range(1, depth)]
-    for device in greet:
-        pl.semaphore_signal(barrier, inc=1, device_id=device, device_id_type=MESH)
+    is_first = (spot == 0) & (level == 0)
+    near = depth - 1
+    far = (spot == plane - 1) & (level >= near)
+    far_devices = [place(k, c, plane - 1) for c in range(near, depth) for k in range(2)]
+    cross_plane = [place(1 - core, level, spot ^ j) for j in range(1, plane)]
+    cross_depth = [place(1 - core, level ^ r, spot) for r in range(1, depth)]
+
+    def greet(devices):
+        for device in devices:
+            pl.semaphore_signal(barrier, inc=1, device_id=device, device_id_type=MESH)
+
+    greet([partner])
+    pl.when(core == 0)(lambda: greet(cross_depth))
+    pl.when(core == 1)(lambda: greet(peers_plane[1:] + cross_plane + peers_depth[1:]))
+    pl.when(is_first & (core == 0))(lambda: greet(far_devices))
 
     left = lax.broadcasted_iota(jnp.int32, (LANES, 2 * LANES), 0)
     right = lax.broadcasted_iota(jnp.int32, (LANES, 2 * LANES), 1)
     had[...] = parity_sign(left & right & (LANES - 1)).astype(jnp.bfloat16)
 
+    for i in range(1, loads):
+        load(i).start()
+
     with jax.named_scope("small_waits"):
         for copy in small:
             copy.wait()
 
-    ahead = 8
-    more = 8
+    ahead = 20
+    more = 16
 
     def turn(line):
         return jnp.broadcast_to(line, (LANES, LANES)).T
@@ -99,7 +111,7 @@
             load(i).wait()
         with jax.named_scope("products"):
             stop = cuts[i + 1]
-            later = stop + more if i + 1 < loads else stop
+            later = stop + more + (4 if not i else 0) if i + 1 < loads else stop
             held = []
             lines = []
             if i == loads - 1:
@@ -161,7 +173,9 @@
                     panel[rows[b], :] = parts[b]
 
     with jax.named_scope("entry_wait"):
-        pl.semaphore_wait(barrier, len(greet))
+        for core_is, expected in ((0, plane), (1, plane + 2 * (depth - 1))):
+            pl.when((core == core_is) & far)(lambda n=expected: pl.semaphore_wait(barrier, n + 1))
+            pl.when((core == core_is) & jnp.logical_not(far))(lambda n=expected: pl.semaphore_wait(barrier, n))
 
     def gather(dst, base, core_to, level_to, spot_to):
         hi_to, lo_to = place(core_to, level_to, spot_to)
@@ -195,6 +209,9 @@
     def to_first(k):
         return remote(first.at[k], got_first.at[k, slot], send_f.at[0], recv_f.at[k], place(1, level, 0))
 
+    def to_first_chip(k):
+        return remote(first.at[k], got_far.at[(level - near) * 2 + core], send_f.at[0], recv_d.at[0], place(k, 0, 0))
+
     def to_head(k):
         return remote(head.at[k], got_head.at[level], send_h.at[0], recv_h.at[0], place(k, 0, 0))
 
@@ -221,7 +238,11 @@
     def send_first():
         for k in range(2):
             gather(first.at[k], 0, k, 0, 0)
-            guarded(jnp.logical_not(reducer), lambda k=k: to_first(k).start())
+            if k:
+                guarded(jnp.logical_not(reducer), lambda: to_first(1).start())
+            else:
+                guarded(jnp.logical_not(reducer | far), lambda: to_first(0).start())
+                guarded(far, lambda: to_first_chip(0).start())
 
     def send_pair(c):
         gather_level(terms.at[c], 1 - core, c)
@@ -248,12 +269,19 @@
 
     def sum_first():
         for k in range(2):
-            with jax.named_scope("first_wait"):
-                received(got_first.at[k, pl.ds(1, 2 * plane - 1)], recv_f.at[k])
-            total = first[k]
-            for i in range(1, 2 * plane):
-                total = total + got_first[k, i]
-            head[k] = total
+            def take(last_slot, k=k):
+                with jax.named_scope("first_wait"):
+                    received(got_first.at[k, pl.ds(1, last_slot - 1)], recv_f.at[k])
+                total = first[k]
+                for i in range(1, last_slot):
+                    total = total + got_first[k, i]
+                head[k] = total
+
+            if k:
+                take(2 * plane)
+            else:
+                guarded(level < near, lambda: take(2 * plane))
+                guarded(level >= near, lambda: take(2 * plane - 2))
             if k:
                 guarded(level != 0, lambda: to_head(1).start())
             else:
@@ -295,16 +323,18 @@
         for c in levels[1:]:
             send_level(c)
 
-    is_first = (spot == 0) & (level == 0)
     others = pl.ds(1, depth - 1)
 
     @pl.when(is_first & (core == 0))
     def _():
         with jax.named_scope("head_wait"):
             received(got_head, recv_h.at[0])
+            received(got_far, recv_d.at[0])
         result = got_head[0]
         for other in range(1, depth):
             result = result + got_head[other]
+        for i in range(len(far_devices)):
+            result = result + got_far[i]
         out_ref[...] = result
 
     @pl.when(is_first & (core == 1))
@@ -393,12 +423,14 @@
             pltpu.VMEM((2, 2 * plane, share, width), f32),
             pltpu.VMEM((2, share, width), f32),
             pltpu.VMEM((depth, share, width), f32),
+            pltpu.VMEM((2, share, width), f32),
             dma((loads,)), dma((3,)),
             dma((1,)), dma((depth,)),
             dma((2,)), dma((2, depth)),
             dma((2,)), dma((1,)),
             dma((1,)), dma((2,)),
             dma((1,)), dma((1,)),
+            dma((1,)),
         ],
         compiler_params=pltpu.CompilerParams(
             collective_id=0, has_side_effects=True, vmem_limit_bytes=60 * 2**20),

time: 14.8 us -> 14.2 us (0.959)
  the two profiles are of different devices: /device:TPU:0 before, /device:TPU:1 now
where the time goes in v6:
time: 14.2 us; the launch traced here: 14.1 us
  Pallas kernels  13.5 us (95%)
  local copies, waits for them, and re-layouts  0.61 us (4%)
    pallas_call x1, Pallas kernels, body(): pl.pallas_call(functools.partial(kernel, hi_count, lo_count), out_shape=p...  13.5 us
    unnamed x1, local copies, waits for them, and re-layouts  0.61 us

profile of v6, /device:TPU:1, one launch (start us, length us, event | category | flops | bytes accessed | tf_op | source)
XLA Modules:
  0.0 14.1 jit_solution(15794852220964405786)
XLA Ops:
  0.0 13.5 %shard_map.37 = f32[32,128]{1,0:T(8,128)S(1)} custom-call(f32[8192,128]{1,0:T(8,128)} %panel_hbm.1, f32[64,128]{1,0:T(8,128)} %bitcast.2, s32[1024]{0:T(1024)} %rows_hbm.1, s32[8,128]{1,0:T(8,128)} %bitcast.3), custom_call_target="tpu_custom_call" | custom-call | flops 1073741824 | bytes 4194304 | tf_op jit(solution)/shard_map/pallas_call | solution.py:402
  13.5 0.6 %copy.5 = f32[32,128]{1,0:T(8,128)} copy(f32[32,128]{1,0:T(8,128)S(1)} %shard_map.37) | data formatting | bytes 32768

commit v7 on v6

--- a/solution.py
+++ b/solution.py
@@ -28,7 +28,7 @@
            panel, signs_ref, rows_ref, picks_ref, field, had, wide, sgn, terms, mine, got_a, got_b, got_c, last,
            first, got_first, head, got_head, got_far,
            load_sem, small_sem, send_a, recv_a, send_b, recv_b, send_c, recv_c,
-           send_f, recv_f, send_h, recv_h, recv_d):
+           send_f, recv_f, send_h, recv_h, recv_d, entered):
     count = panel.shape[0]
     share = out_ref.shape[0]
     kept = rows_ref.shape[0]
@@ -70,15 +70,27 @@
     far = (spot == plane - 1) & (level >= near)
     far_devices = [place(k, c, plane - 1) for c in range(near, depth) for k in range(2)]
     cross_plane = [place(1 - core, level, spot ^ j) for j in range(1, plane)]
-    cross_depth = [place(1 - core, level ^ r, spot) for r in range(1, depth)]
-
-    def greet(devices):
+    cross_depth = [place(1 - core, level ^ r, spot) for r in range(depth)]
+
+    def greet(devices, semaphore=barrier):
         for device in devices:
-            pl.semaphore_signal(barrier, inc=1, device_id=device, device_id_type=MESH)
+            pl.semaphore_signal(semaphore, inc=1, device_id=device, device_id_type=MESH)
+
+    def greet_depth(devices, wanted, semaphore=barrier):
+        for r in range(1, depth):
+            pl.when(wanted(level ^ r))(lambda r=r: greet([peers[r] for peers in devices], semaphore))
 
     greet([partner])
-    pl.when(core == 0)(lambda: greet(cross_depth))
-    pl.when(core == 1)(lambda: greet(peers_plane[1:] + cross_plane + peers_depth[1:]))
+
+    @pl.when(core == 0)
+    def _():
+        greet_depth([cross_depth], lambda other: other > level)
+
+    @pl.when(core == 1)
+    def _():
+        greet(peers_plane[1:] + cross_plane)
+        greet_depth([peers_depth, cross_depth], lambda other: other > level)
+
     pl.when(is_first & (core == 0))(lambda: greet(far_devices))
 
     left = lax.broadcasted_iota(jnp.int32, (LANES, 2 * LANES), 0)
@@ -173,9 +185,17 @@
                     panel[rows[b], :] = parts[b]
 
     with jax.named_scope("entry_wait"):
-        for core_is, expected in ((0, plane), (1, plane + 2 * (depth - 1))):
+        for core_is, expected in ((0, plane + level), (1, plane + 2 * level)):
             pl.when((core == core_is) & far)(lambda n=expected: pl.semaphore_wait(barrier, n + 1))
             pl.when((core == core_is) & jnp.logical_not(far))(lambda n=expected: pl.semaphore_wait(barrier, n))
+
+    @pl.when(core == 0)
+    def _():
+        greet_depth([cross_depth], lambda other: other < level, entered.at[0])
+
+    @pl.when(core == 1)
+    def _():
+        greet_depth([peers_depth], lambda other: other < level, entered.at[0])
 
     def gather(dst, base, core_to, level_to, spot_to):
         hi_to, lo_to = place(core_to, level_to, spot_to)
@@ -261,7 +281,7 @@
             else:
                 guarded(core == 0, lambda: to_plane(c, 0).start())
 
-        for j in list(range(1, plane)) + [0]:
+        for j in list(range(plane - 1, -1, -1)):
             if c:
                 part_sum(j)
             else:
@@ -316,6 +336,8 @@
             send_pair(c + lead)
 
     guarded(reducer, sum_first)
+    above = 2 * (depth - 1 - level)
+    guarded((core == 1) & (above > 0), lambda: pl.semaphore_wait(entered.at[0], above))
     guarded((core == 1) & (spot != 0), lambda: send_level(0))
 
     @pl.when(core == 1)
@@ -430,7 +452,7 @@
             dma((2,)), dma((1,)),
             dma((1,)), dma((2,)),
             dma((1,)), dma((1,)),
-            dma((1,)),
+            dma((1,)), pltpu.SemaphoreType.REGULAR((1,)),
         ],
         compiler_params=pltpu.CompilerParams(
             collective_id=0, has_side_effects=True, vmem_limit_bytes=60 * 2**20),

time: 14.2 us -> 14.1 us (level)
  Pallas kernels: 13.5 us -> 13.3 us
    pallas_call x1, Pallas kernels: 13.5 us -> 13.3 us  [body(): pl.pallas_call(functools.partial(kernel, hi_count, lo_count), out_shape=p...]
where the time goes in v7:
time: 14.1 us; the launch traced here: 13.9 us
  Pallas kernels  13.3 us (94%)
  local copies, waits for them, and re-layouts  0.61 us (4%)
    pallas_call x1, Pallas kernels, body(): pl.pallas_call(functools.partial(kernel, hi_count, lo_count), out_shape=p...  13.3 us
    unnamed x1, local copies, waits for them, and re-layouts  0.61 us

profile of v7, /device:TPU:1, one launch (start us, length us, event | category | flops | bytes accessed | tf_op | source)
XLA Modules:
  0.0 13.9 jit_solution(16758111030349395408)
XLA Ops:
  0.0 13.3 %shard_map.37 = f32[32,128]{1,0:T(8,128)S(1)} custom-call(f32[8192,128]{1,0:T(8,128)} %panel_hbm.1, f32[64,128]{1,0:T(8,128)} %bitcast.2, s32[1024]{0:T(1024)} %rows_hbm.1, s32[8,128]{1,0:T(8,128)} %bitcast.3), custom_call_target="tpu_custom_call" | custom-call | flops 1073741824 | bytes 4194304 | tf_op jit(solution)/shard_map/pallas_call | solution.py:424
  13.3 0.6 %copy.5 = f32[32,128]{1,0:T(8,128)} copy(f32[32,128]{1,0:T(8,128)S(1)} %shard_map.37) | data formatting | bytes 32768

commit v8 on v7

--- a/solution.py
+++ b/solution.py
@@ -27,8 +27,8 @@
 def kernel(hi_count, lo_count, panel_hbm, signs_hbm, rows_hbm, picks_hbm, out_ref,
            panel, signs_ref, rows_ref, picks_ref, field, had, wide, sgn, terms, mine, got_a, got_b, got_c, last,
            first, got_first, head, got_head, got_far,
-           load_sem, small_sem, send_a, recv_a, send_b, recv_b, send_c, recv_c,
-           send_f, recv_f, send_h, recv_h, recv_d, entered):
+           load_sem, small_sem, send, recv_a, recv_b, recv_c,
+           recv_f, recv_h, recv_d, entered):
     count = panel.shape[0]
     share = out_ref.shape[0]
     kept = rows_ref.shape[0]
@@ -216,9 +216,9 @@
                 def _():
                     gather(dst, j * share, core_to, level_to, spot ^ j)
 
-    def remote(src, dst, send, recv, device):
+    def remote(src, dst, done, recv, device):
         return pltpu.make_async_remote_copy(
-            src_ref=src, dst_ref=dst, send_sem=send, recv_sem=recv,
+            src_ref=src, dst_ref=dst, send_sem=done, recv_sem=recv,
             device_id=device, device_id_type=MESH)
 
     levels = range(depth)
@@ -227,30 +227,27 @@
     slot = (spot * 2 + core) ^ 1
 
     def to_first(k):
-        return remote(first.at[k], got_first.at[k, slot], send_f.at[0], recv_f.at[k], place(1, level, 0))
+        return remote(first.at[k], got_first.at[k, slot], send.at[0], recv_f.at[k], place(1, level, 0))
 
     def to_first_chip(k):
-        return remote(first.at[k], got_far.at[(level - near) * 2 + core], send_f.at[0], recv_d.at[0], place(k, 0, 0))
+        return remote(first.at[k], got_far.at[(level - near) * 2 + core], send.at[0], recv_d.at[0], place(k, 0, 0))
 
     def to_head(k):
-        return remote(head.at[k], got_head.at[level], send_h.at[0], recv_h.at[0], place(k, 0, 0))
+        return remote(head.at[k], got_head.at[level], send.at[0], recv_h.at[0], place(k, 0, 0))
 
     def to_partner(c):
-        return remote(terms.at[c], got_a.at[c], send_a.at[0], recv_a.at[c], partner)
+        return remote(terms.at[c], got_a.at[c], send.at[0], recv_a.at[c], partner)
 
     def to_plane(c, j):
         part = pl.ds(j * share, share)
-        return remote(mine.at[c, part], got_b.at[core, c, part], send_b.at[min(c, 1)], recv_b.at[core, c],
+        return remote(mine.at[c, part], got_b.at[core, c, part], send.at[0], recv_b.at[core, c],
                       place(1, level, spot ^ j))
 
     def to_level(k, c):
-        return remote(last.at[k, c], got_c.at[level], send_c.at[k], recv_c.at[0], place(k, c, spot))
+        return remote(last.at[k, c], got_c.at[level], send.at[0], recv_c.at[0], place(k, c, spot))
 
     def received(ref, recv):
-        remote(ref, ref, send_f.at[0], recv, partner).wait_recv()
-
-    def sent(ref, send):
-        remote(ref, ref, send, recv_f.at[0], partner).wait_send()
+        remote(ref, ref, send.at[0], recv, partner).wait_recv()
 
     def guarded(condition, action):
         pl.when(condition)(action)
@@ -386,26 +383,15 @@
             result = result + got_c[level ^ r]
         out_ref[...] = result
 
-    guarded(jnp.logical_not(reducer), lambda: sent(first, send_f.at[0]))
-    guarded(reducer & (level != 0), lambda: sent(head, send_h.at[0]))
-    guarded(reducer & (level == 0), lambda: to_head(0).wait_send())
-    sent(terms, send_a.at[0])
-
-    @pl.when(core == 0)
-    def _():
-        sent(mine.at[others], send_b.at[1])
-        sent(mine.at[0, pl.ds(0, (plane - 1) * share)], send_b.at[0])
-
-    @pl.when(core == 1)
-    def _():
-        sent(mine.at[others, pl.ds(share, (plane - 1) * share)], send_b.at[1])
-        guarded(spot == 0, lambda: sent(mine.at[0, pl.ds(0, (plane - 1) * share)], send_b.at[0]))
-        guarded(spot != 0, lambda: sent(mine.at[0, pl.ds(0, (plane - 2) * share)], send_b.at[0]))
-        guarded(spot == 0, lambda: sent(last.at[0, others], send_c.at[0]))
-        guarded(spot != 0, lambda: sent(last.at[0], send_c.at[0]))
-        fewer = (spot == 0) & (level != 0)
-        guarded(fewer, lambda: sent(last.at[1, pl.ds(0, depth - 2)], send_c.at[1]))
-        guarded(jnp.logical_not(fewer), lambda: sent(last.at[1, others], send_c.at[1]))
+    def all_sent(blocks):
+        ref = panel.at[pl.ds(0, blocks * share)]
+        remote(ref, ref, send.at[0], recv_d.at[0], partner).wait_send()
+
+    pairs = plane * depth
+    onward = plane + 2 * (depth - 1)
+    pl.when(core == 0)(lambda: all_sent(2 * pairs + 1))
+    guarded((core == 1) & (spot == 0), lambda: all_sent(2 * pairs - plane - depth + 1 + onward))
+    guarded((core == 1) & (spot != 0), lambda: all_sent(2 * pairs - plane - depth + 1 + onward + 1))
 
 
 def body(panel, row_signs, sample_rows):
@@ -447,12 +433,8 @@
             pltpu.VMEM((depth, share, width), f32),
             pltpu.VMEM((2, share, width), f32),
             dma((loads,)), dma((3,)),
-            dma((1,)), dma((depth,)),
-            dma((2,)), dma((2, depth)),
-            dma((2,)), dma((1,)),
-            dma((1,)), dma((2,)),
-            dma((1,)), dma((1,)),
-            dma((1,)), pltpu.SemaphoreType.REGULAR((1,)),
+            dma((1,)), dma((depth,)), dma((2, depth)), dma((1,)),
+            dma((2,)), dma((1,)), dma((1,)), pltpu.SemaphoreType.REGULAR((1,)),
         ],
         compiler_params=pltpu.CompilerParams(
             collective_id=0, has_side_effects=True, vmem_limit_bytes=60 * 2**20),

time: 14.1 us -> 14 us (level)
  no operation moved by 1% of the time
where the time goes in v8:
time: 14 us; the launch traced here: 13.9 us
  Pallas kernels  13.3 us (95%)
  local copies, waits for them, and re-layouts  0.61 us (4%)
    pallas_call x1, Pallas kernels, body(): pl.pallas_call(functools.partial(kernel, hi_count, lo_count), out_shape=p...  13.3 us
    unnamed x1, local copies, waits for them, and re-layouts  0.61 us

profile of v8, /device:TPU:1, one launch (start us, length us, event | category | flops | bytes accessed | tf_op | source)
XLA Modules:
  0.0 13.9 jit_solution(3895928276564431620)
XLA Ops:
  0.0 13.3 %shard_map.37 = f32[32,128]{1,0:T(8,128)S(1)} custom-call(f32[8192,128]{1,0:T(8,128)} %panel_hbm.1, f32[64,128]{1,0:T(8,128)} %bitcast.2, s32[1024]{0:T(1024)} %rows_hbm.1, s32[8,128]{1,0:T(8,128)} %bitcast.3), custom_call_target="tpu_custom_call" | custom-call | flops 1073741824 | bytes 4194304 | tf_op jit(solution)/shard_map/pallas_call | solution.py:410
  13.3 0.6 %copy.5 = f32[32,128]{1,0:T(8,128)} copy(f32[32,128]{1,0:T(8,128)S(1)} %shard_map.37) | data formatting | bytes 32768

commit v9 on v8

--- a/solution.py
+++ b/solution.py
@@ -67,8 +67,8 @@
     barrier = pltpu.get_barrier_semaphore()
     is_first = (spot == 0) & (level == 0)
     near = depth - 1
-    far = (spot == plane - 1) & (level >= near)
-    far_devices = [place(k, c, plane - 1) for c in range(near, depth) for k in range(2)]
+    far = (core == 0) & (spot == plane - 1) & (level >= near)
+    far_devices = [place(0, c, plane - 1) for c in range(near, depth)]
     cross_plane = [place(1 - core, level, spot ^ j) for j in range(1, plane)]
     cross_depth = [place(1 - core, level ^ r, spot) for r in range(depth)]
 
@@ -91,7 +91,7 @@
         greet(peers_plane[1:] + cross_plane)
         greet_depth([peers_depth, cross_depth], lambda other: other > level)
 
-    pl.when(is_first & (core == 0))(lambda: greet(far_devices))
+    pl.when(is_first)(lambda: greet(far_devices))
 
     left = lax.broadcasted_iota(jnp.int32, (LANES, 2 * LANES), 0)
     right = lax.broadcasted_iota(jnp.int32, (LANES, 2 * LANES), 1)
@@ -186,7 +186,7 @@
 
     with jax.named_scope("entry_wait"):
         for core_is, expected in ((0, plane + level), (1, plane + 2 * level)):
-            pl.when((core == core_is) & far)(lambda n=expected: pl.semaphore_wait(barrier, n + 1))
+            pl.when((core == core_is) & far)(lambda n=expected: pl.semaphore_wait(barrier, n + 2))
             pl.when((core == core_is) & jnp.logical_not(far))(lambda n=expected: pl.semaphore_wait(barrier, n))
 
     @pl.when(core == 0)
@@ -230,7 +230,7 @@
         return remote(first.at[k], got_first.at[k, slot], send.at[0], recv_f.at[k], place(1, level, 0))
 
     def to_first_chip(k):
-        return remote(first.at[k], got_far.at[(level - near) * 2 + core], send.at[0], recv_d.at[0], place(k, 0, 0))
+        return remote(first.at[k], got_far.at[level - near], send.at[0], recv_d.at[0], place(k, 0, 0))
 
     def to_head(k):
         return remote(head.at[k], got_head.at[level], send.at[0], recv_h.at[0], place(k, 0, 0))
@@ -255,11 +255,8 @@
     def send_first():
         for k in range(2):
             gather(first.at[k], 0, k, 0, 0)
-            if k:
-                guarded(jnp.logical_not(reducer), lambda: to_first(1).start())
-            else:
-                guarded(jnp.logical_not(reducer | far), lambda: to_first(0).start())
-                guarded(far, lambda: to_first_chip(0).start())
+            guarded(jnp.logical_not(reducer | far), lambda k=k: to_first(k).start())
+            guarded(far, lambda k=k: to_first_chip(k).start())
 
     def send_pair(c):
         gather_level(terms.at[c], 1 - core, c)
@@ -294,11 +291,8 @@
                     total = total + got_first[k, i]
                 head[k] = total
 
-            if k:
-                take(2 * plane)
-            else:
-                guarded(level < near, lambda: take(2 * plane))
-                guarded(level >= near, lambda: take(2 * plane - 2))
+            guarded(level < near, lambda: take(2 * plane))
+            guarded(level >= near, lambda: take(2 * plane - 1))
             if k:
                 guarded(level != 0, lambda: to_head(1).start())
             else:
@@ -360,9 +354,12 @@
     def _():
         with jax.named_scope("head_wait"):
             received(got_head.at[others], recv_h.at[0])
+            received(got_far, recv_d.at[0])
         result = head[1]
         for other in range(1, depth):
             result = result + got_head[other]
+        for i in range(len(far_devices)):
+            result = result + got_far[i]
         out_ref[...] = result
 
     @pl.when(jnp.logical_not(is_first) & (core == 0))
@@ -431,7 +428,7 @@
             pltpu.VMEM((2, 2 * plane, share, width), f32),
             pltpu.VMEM((2, share, width), f32),
             pltpu.VMEM((depth, share, width), f32),
-            pltpu.VMEM((2, share, width), f32),
+            pltpu.VMEM((1, share, width), f32),
             dma((loads,)), dma((3,)),
             dma((1,)), dma((depth,)), dma((2, depth)), dma((1,)),
             dma((2,)), dma((1,)), dma((1,)), pltpu.SemaphoreType.REGULAR((1,)),

time: 14 us -> 14 us (level)
  the two profiles are of different devices: /device:TPU:1 before, /device:TPU:0 now
where the time goes in v9:
time: 14 us; the launch traced here: 13.8 us
  Pallas kernels  13.2 us (94%)
  local copies, waits for them, and re-layouts  0.61 us (4%)
    pallas_call x1, Pallas kernels, body(): pl.pallas_call(functools.partial(kernel, hi_count, lo_count), out_shape=p...  13.2 us
    unnamed x1, local copies, waits for them, and re-layouts  0.61 us

profile of v9, /device:TPU:0, one launch (start us, length us, event | category | flops | bytes accessed | tf_op | source)
XLA Modules:
  0.0 13.8 jit_solution(8471741609216311100)
XLA Ops:
  0.0 13.2 %shard_map.37 = f32[32,128]{1,0:T(8,128)S(1)} custom-call(f32[8192,128]{1,0:T(8,128)} %panel_hbm.1, f32[64,128]{1,0:T(8,128)} %bitcast.2, s32[1024]{0:T(1024)} %rows_hbm.1, s32[8,128]{1,0:T(8,128)} %bitcast.3), custom_call_target="tpu_custom_call" | custom-call | flops 1073741824 | bytes 4194304 | tf_op jit(solution)/shard_map/pallas_call | solution.py:407
  13.2 0.6 %copy.5 = f32[32,128]{1,0:T(8,128)} copy(f32[32,128]{1,0:T(8,128)S(1)} %shard_map.37) | data formatting | bytes 32768

commit v10 on v9

--- a/solution.py
+++ b/solution.py
@@ -93,12 +93,12 @@
 
     pl.when(is_first)(lambda: greet(far_devices))
 
+    for i in range(1, loads):
+        load(i).start()
+
     left = lax.broadcasted_iota(jnp.int32, (LANES, 2 * LANES), 0)
     right = lax.broadcasted_iota(jnp.int32, (LANES, 2 * LANES), 1)
     had[...] = parity_sign(left & right & (LANES - 1)).astype(jnp.bfloat16)
-
-    for i in range(1, loads):
-        load(i).start()
 
     with jax.named_scope("small_waits"):
         for copy in small:

time: 14 us -> 14 us (level)
  no operation moved by 1% of the time
where the time goes in v10:
time: 14 us; the launch traced here: 13.8 us
  Pallas kernels  13.2 us (94%)
  local copies, waits for them, and re-layouts  0.61 us (4%)
    pallas_call x1, Pallas kernels, body(): pl.pallas_call(functools.partial(kernel, hi_count, lo_count), out_shape=p...  13.2 us
    unnamed x1, local copies, waits for them, and re-layouts  0.61 us

profile of v10, /device:TPU:0, one launch (start us, length us, event | category | flops | bytes accessed | tf_op | source)
XLA Modules:
  0.0 13.8 jit_solution(2451555887561276288)
XLA Ops:
  0.0 13.2 %shard_map.37 = f32[32,128]{1,0:T(8,128)S(1)} custom-call(f32[8192,128]{1,0:T(8,128)} %panel_hbm.1, f32[64,128]{1,0:T(8,128)} %bitcast.2, s32[1024]{0:T(1024)} %rows_hbm.1, s32[8,128]{1,0:T(8,128)} %bitcast.3), custom_call_target="tpu_custom_call" | custom-call | flops 1073741824 | bytes 4194304 | tf_op jit(solution)/shard_map/pallas_call | solution.py:407
  13.2 0.6 %copy.5 = f32[32,128]{1,0:T(8,128)} copy(f32[32,128]{1,0:T(8,128)S(1)} %shard_map.37) | data formatting | bytes 32768

commit v11 on v10

--- a/solution.py
+++ b/solution.py
@@ -166,7 +166,7 @@
     with jax.named_scope("butterflies"):
         steps = groups // FUSED
         tiles = FUSED * LANES // TILE
-        lines = 8
+        lines = 4
 
         @pl.loop(0, lines)
         def _(g):

time: 14 us -> 13.9 us (level)
  no operation moved by 1% of the time
where the time goes in v11:
time: 13.9 us; the launch traced here: 13.8 us
  Pallas kernels  13.2 us (95%)
  local copies, waits for them, and re-layouts  0.61 us (4%)
    pallas_call x1, Pallas kernels, body(): pl.pallas_call(functools.partial(kernel, hi_count, lo_count), out_shape=p...  13.2 us
    unnamed x1, local copies, waits for them, and re-layouts  0.61 us

profile of v11, /device:TPU:0, one launch (start us, length us, event | category | flops | bytes accessed | tf_op | source)
XLA Modules:
  0.0 13.8 jit_solution(15123625751073636246)
XLA Ops:
  0.0 13.2 %shard_map.37 = f32[32,128]{1,0:T(8,128)S(1)} custom-call(f32[8192,128]{1,0:T(8,128)} %panel_hbm.1, f32[64,128]{1,0:T(8,128)} %bitcast.2, s32[1024]{0:T(1024)} %rows_hbm.1, s32[8,128]{1,0:T(8,128)} %bitcast.3), custom_call_target="tpu_custom_call" | custom-call | flops 1073741824 | bytes 4194304 | tf_op jit(solution)/shard_map/pallas_call | solution.py:407
  13.2 0.6 %copy.5 = f32[32,128]{1,0:T(8,128)} copy(f32[32,128]{1,0:T(8,128)S(1)} %shard_map.37) | data formatting | bytes 32768
